TPU v7x, 512 devices: a whole 4x4x16 slice. The times are simulated.
512 devices in a mesh: vocab: 32 (over x, y, core), dp: 16 (over z).
Axes of the slice: x: 4, y: 4, z: 16, core: 2. Of those that a mesh axis runs over, the one named last changes fastest.
Arguments:
- hidden: bfloat16 [2048, 2048], P('dp', 'vocab')
- head_weight: bfloat16 [2048, 65536], P('dp', 'vocab')
- teacher_logits: bfloat16 [2048, 65536], P('dp', 'vocab')
- target_ids: int32 [2048], P('dp'), may hold values from 0 to 65535
- segment_ids: int32 [16, 128], P('dp'), may hold values from 0 to 15, never falling along the last dimension, each value on 1 to 16 neighbouring positions
- pair_order: int32 [16, 16], P('dp'), may hold values from 0 to 15, each once within a row
Outputs:
- hidden_grad: bfloat16 [2048, 2048], P('dp', 'vocab')
- head_grad: float32 [2048, 65536], P('dp', 'vocab')
- loss: float32 [], replicated
Inputs may be any that keep to these rules, and one draw needn't show every extreme that they name: `segment_ids`: in each group the row's sequence number never falls along the rows, and every sequence has 1 to 16 rows. `pair_order`: each group's row is a permutation of its 16 sequences; pair p is entry 2p (chosen) and entry 2p + 1 (rejected).
All inputs are finite; a program needn't handle non-finite values.
Results may differ from a plain program's by a relative error of at most 0.018.
Values may be sent and summed in bfloat16 or wider, within the bound.
No kernel may reach another device: no remote copies, remote signals or barrier semaphores. Data moves between devices by JAX's collectives and lax.ppermute only.
A program may use at most 64 MiB of HBM per device.

v0:
```python
import jax
import jax.numpy as jnp
from jax import lax
from jax.sharding import PartitionSpec as P

dpo_beta = 0.1
dpo_gamma = 4.0


def pair_weights(log_ratio, segments, ordering):
    seq_count = ordering.shape[0]
    labels = lax.broadcasted_iota(jnp.int32, (1, seq_count), 1)
    seq_hot = (segments[:, None] == labels).astype(jnp.float32)
    seq_ratio = jnp.sum(seq_hot * log_ratio[:, None], axis=0)
    chosen = ordering[0::2]
    rejected = ordering[1::2]
    chosen_hot = (chosen[:, None] == labels).astype(jnp.float32)
    rejected_hot = (rejected[:, None] == labels).astype(jnp.float32)
    margin = dpo_beta * (
        jnp.sum(chosen_hot * seq_ratio[None, :], axis=1)
        - jnp.sum(rejected_hot * seq_ratio[None, :], axis=1)
    )
    strength = dpo_gamma * dpo_beta * jax.nn.sigmoid(-margin)
    coeffs = jnp.sum((rejected_hot - chosen_hot) * strength[:, None], axis=0)
    row_weight = jnp.sum(seq_hot * coeffs[None, :], axis=1)
    return (row_weight, jnp.sum(jax.nn.softplus(-margin)))


def to_all(block, axis):
    count = lax.axis_size(axis)
    copies = jnp.broadcast_to(block[None], (count,) + block.shape)
    return lax.all_to_all(copies, axis, 0, 0, tiled=True)


def on_device(hidden, head_weight, teacher_logits, target_ids, segment_ids, pair_order):
    f32, bf16 = (jnp.float32, jnp.bfloat16)
    rows_full = lax.all_gather(hidden, "vocab", axis=1, tiled=True)
    width = head_weight.shape[1]
    half = width // 2
    weight_lo = lax.all_gather(head_weight[:, :half], "dp", axis=0, tiled=True)
    weight_hi = lax.all_gather(head_weight[:, half:], "dp", axis=0, tiled=True)
    student = jnp.concatenate(
        [
            jnp.dot(rows_full, weight_lo, preferred_element_type=f32),
            jnp.dot(rows_full, weight_hi, preferred_element_type=f32),
        ],
        axis=1,
    )
    teacher = teacher_logits.astype(f32)
    n_vocab = lax.axis_size("vocab")
    n_dp = lax.axis_size("dp")
    rows = student.shape[0]
    offset = lax.axis_index("vocab") * width
    column = lax.broadcasted_iota(jnp.int32, student.shape, 1) + offset
    is_target = column == target_ids[:, None]
    own_max = jnp.max(student, axis=1)
    own_tmax = jnp.max(teacher, axis=1)
    own_exp = jnp.exp(student - own_max[:, None])
    own_texp = jnp.exp(teacher - own_tmax[:, None])
    stats = jnp.stack(
        [
            own_max,
            own_tmax,
            jnp.sum(own_exp, axis=1),
            jnp.sum(own_texp, axis=1),
            jnp.sum(own_texp * (teacher - student), axis=1),
            jnp.sum(jnp.where(is_target, student, 0.0), axis=1),
            jnp.sum(jnp.where(is_target, teacher, 0.0), axis=1),
            jnp.zeros((rows,), f32),
        ]
    )
    every = to_all(stats, "vocab").reshape(n_vocab, 8, rows)
    max_student = jnp.max(every[:, 0], axis=0)
    max_teacher = jnp.max(every[:, 1], axis=0)
    scale_s = jnp.exp(every[:, 0] - max_student[None])
    scale_t = jnp.exp(every[:, 1] - max_teacher[None])
    sum_student = jnp.sum(every[:, 2] * scale_s, axis=0)
    sum_teacher = jnp.sum(every[:, 3] * scale_t, axis=0)
    cross = jnp.sum(every[:, 4] * scale_t, axis=0)
    target_student = jnp.sum(every[:, 5], axis=0)
    target_teacher = jnp.sum(every[:, 6], axis=0)
    lse_student = max_student + jnp.log(sum_student)
    lse_teacher = max_teacher + jnp.log(sum_teacher)
    kl_rows = cross / sum_teacher - lse_teacher + lse_student
    log_ratio = target_student - lse_student - (target_teacher - lse_teacher)
    row_weight, dpo_sum = pair_weights(log_ratio, segment_ids[0], pair_order[0])
    group_objective = jnp.sum(kl_rows) + dpo_gamma * dpo_sum
    exp_student = jnp.exp(student - max_student[:, None])
    exp_teacher = jnp.exp(teacher - max_teacher[:, None])
    prob_student = exp_student / sum_student[:, None]
    prob_teacher = exp_teacher / sum_teacher[:, None]
    logit_grad = (
        prob_student - prob_teacher + row_weight[:, None] * (is_target.astype(f32) - prob_student)
    ).astype(bf16)
    grad_lo = logit_grad[:, :half]
    grad_hi = logit_grad[:, half:]
    all_lo = lax.all_gather(grad_lo, "dp", axis=0, tiled=True)
    all_hi = lax.all_gather(grad_hi, "dp", axis=0, tiled=True)
    nt = (((1,), (1,)), ((), ()))
    hidden_term = (
        lax.dot_general(grad_lo, weight_lo, nt, preferred_element_type=f32)
        + lax.dot_general(grad_hi, weight_hi, nt, preferred_element_type=f32)
    ).astype(bf16)
    feats = hidden_term.shape[1] // n_vocab
    terms = hidden_term.reshape(rows, n_vocab, feats).swapaxes(0, 1)
    terms = lax.all_to_all(terms, "vocab", 0, 0, tiled=True)
    hidden_grad = jnp.sum(terms.astype(f32), axis=0).astype(bf16)
    objectives = to_all(jnp.full((8, 128), group_objective, f32), "dp").reshape(n_dp, 8, 128)
    loss_value = jnp.sum(objectives[:, 0, 0]) / (rows * n_dp)
    grad_cols = lax.all_to_all(rows_full, "dp", split_axis=1, concat_axis=0, tiled=True)
    tn = (((0,), (0,)), ((), ()))
    head_grad = jnp.concatenate(
        [
            lax.dot_general(grad_cols, all_lo, tn, preferred_element_type=f32),
            lax.dot_general(grad_cols, all_hi, tn, preferred_element_type=f32),
        ],
        axis=1,
    )
    return (hidden_grad, head_grad, loss_value)


def solution(mesh):
    return jax.shard_map(
        on_device,
        mesh=mesh,
        in_specs=(
            P("dp", "vocab"),
            P("dp", "vocab"),
            P("dp", "vocab"),
            P("dp"),
            P("dp", None),
            P("dp", None),
        ),
        out_specs=(P("dp", "vocab"), P("dp", "vocab"), P()),
        check_vma=False,
    )
```

profile of v0, /device:TPU:2, one launch (start us, length us, event | category | flops | bytes accessed | tf_op | source)
XLA Modules:
  0.0 374.6 jit_solution(1377167011678018934)
XLA Ops:
  7.2 0.0 all-gather.5.cloned.1.call-start
  7.2 1.8 fusion.19
  9.0 0.0 all-gather.5.cloned.1.call-update
  9.1 0.0 all-gather.7.cloned.1.call-start
  9.1 0.7 all-gather.7.cloned.1.call-update
  9.8 1.2 reduce_max.71
  11.0 29.9 %all_gather.15 = bf16[128,2048]{0,1:T(8,128)(2,1)} all-gather(bf16[128,64]{0,1:T(8,128)(2,1)} %param.6), channel_id=1, replica_groups=mesh['vocab'=32,'dp'=16] {'vocab'}, dimensions={1}, use_global_device_ids=true | all-gather | bytes 540672 | tf_op jit(solution)/shard_map/all_gather | solution.py:37
  40.9 52.3 %all-gather.5.cloned.1.call-done = bf16[2048,1024]{1,0:T(8,128)(2,1)} async-done(((bf16[128,1024]{1,0:T(8,128)(2,1)}), bf16[2048,1024]{1,0:T(8,128)(2,1)}) %all-gather.5.cloned.1.call-update) | async-done | bytes 4194320 | tf_op jit(solution)/shard_map/all_gather | solution.py:40
  93.3 3.2 fusion.22
  96.5 74.8 %all-gather.7.cloned.1.call-done = bf16[2048,1024]{1,0:T(8,128)(2,1)} async-done(((bf16[128,1024]{1,0:T(8,128)(2,1)}), bf16[2048,1024]{1,0:T(8,128)(2,1)}) %all-gather.7.cloned.1.call-update) | async-done | bytes 4194320 | tf_op jit(solution)/shard_map/all_gather | solution.py:41
  171.3 3.2 fusion.23
  174.5 0.8 fusion.1
  175.4 0.7 broadcast_in_dim.8
  176.0 7.4 %all-to-all-start = ((f32[32,8,128]{2,1,0:T(8,128)}), f32[32,8,128]{2,1,0:T(8,128)S(1)}, u32[]{:S(2)}, u32[]{:S(2)}) async-start(f32[32,8,128]{2,1,0:T(8,128)} %broadcast_in_dim.8), calls=%async_computation | async-start | bytes 262144 | tf_op jit(solution)/shard_map/all_to_all | solution.py:32
  183.5 0.0 all-gather.9.cloned.1.call-start
  183.5 0.1 slice.51
  183.6 0.1 slice.50
  183.7 6.4 %all-to-all-done = f32[32,8,128]{2,1,0:T(8,128)S(1)} async-done(((f32[32,8,128]{2,1,0:T(8,128)}), f32[32,8,128]{2,1,0:T(8,128)S(1)}, u32[]{:S(2)}, u32[]{:S(2)}) %all-to-all-start) | async-done | bytes 131104 | tf_op jit(solution)/shard_map/all_to_all | solution.py:32
  190.1 0.1 fusion.20
  190.3 0.6 add_reduce_fusion
  190.9 0.1 select_reduce_fusion.1
  191.0 0.2 select_reduce_fusion.2
  191.3 0.6 fusion.14
  191.9 0.1 multiply_reduce_fusion.3
  192.0 0.1 select_reduce_fusion
  192.1 0.6 fusion.5
  192.7 0.9 fusion.18
  193.6 0.0 all-gather.11.cloned.1.call-start
  193.6 0.5 all-gather.11.cloned.1.call-update
  194.1 7.4 %all-to-all-start.2 = ((bf16[128,16,128]{0,2,1:T(8,128)(2,1)}), bf16[128,16,128]{0,2,1:T(8,128)(2,1)S(1)}, u32[]{:S(2)}, u32[]{:S(2)}) async-start(bf16[128,16,128]{0,2,1:T(8,128)(2,1)} %bitcast.17), calls=%async_computation.2 | async-start | bytes 1048576 | tf_op jit(solution)/shard_map/all_to_all | solution.py:110
  202.9 3.8 %fusion.16 = f32[128,2048]{1,0:T(8,128)S(1)} fusion(bf16[2048,1024]{1,0:T(8,128)(2,1)} %all-gather.5.cloned.1.call-done, bf16[128,2048]{1,0:T(8,128)(2,1)S(1)} %fusion.5), kind=kOutput, calls=%fused_computation.50 | convolution fusion | flops 536870912 | bytes 5505024 | tf_op jit(solution)/shard_map/dot_general | solution.py:101
  206.7 29.5 %all-to-all-done.2 = bf16[128,16,128]{0,2,1:T(8,128)(2,1)S(1)} async-done(((bf16[128,16,128]{0,2,1:T(8,128)(2,1)}), bf16[128,16,128]{0,2,1:T(8,128)(2,1)S(1)}, u32[]{:S(2)}, u32[]{:S(2)}) %all-to-all-start.2) | async-done | bytes 524320 | tf_op jit(solution)/shard_map/all_to_all | solution.py:110
  236.2 0.6 broadcast_in_dim_broadcast_in_dim_broadcast_in_dim.3
  236.8 6.4 %all-to-all-start.3 = ((f32[16,8,128]{2,1,0:T(8,128)}), f32[16,8,128]{2,1,0:T(8,128)S(1)}, u32[]{:S(2)}, u32[]{:S(2)}) async-start(f32[16,8,128]{2,1,0:T(8,128)} %broadcast_in_dim_broadcast_in_dim_broadcast_in_dim.3), calls=%async_computation.3 | async-start | bytes 131072 | tf_op jit(solution)/shard_map/all_to_all | solution.py:32
  243.2 3.7 fusion
  246.9 1.0 copy.32
  247.9 8.8 %all-to-all-done.3 = f32[16,8,128]{2,1,0:T(8,128)S(1)} async-done(((f32[16,8,128]{2,1,0:T(8,128)}), f32[16,8,128]{2,1,0:T(8,128)S(1)}, u32[]{:S(2)}, u32[]{:S(2)}) %all-to-all-start.3) | async-done | bytes 65568 | tf_op jit(solution)/shard_map/all_to_all | solution.py:32
  256.8 5.0 %all-to-all-start.1 = ((bf16[32,128,64]{1,2,0:T(8,128)(2,1)}), bf16[32,128,64]{1,2,0:T(8,128)(2,1)S(1)}, u32[]{:S(2)}, u32[]{:S(2)}) async-start(bf16[32,128,64]{1,2,0:T(8,128)(2,1)} %bitcast.16), calls=%async_computation.1 | async-start | bytes 1048576 | tf_op jit(solution)/shard_map/all_to_all | solution.py:106
  261.8 0.3 copy.33
  262.1 0.6 slice_reduce_fusion
  263.4 8.2 %all-to-all-done.1 = bf16[32,128,64]{1,2,0:T(8,128)(2,1)S(1)} async-done(((bf16[32,128,64]{1,2,0:T(8,128)(2,1)}), bf16[32,128,64]{1,2,0:T(8,128)(2,1)S(1)}, u32[]{:S(2)}, u32[]{:S(2)}) %all-to-all-start.1) | async-done | bytes 524320 | tf_op jit(solution)/shard_map/all_to_all | solution.py:106
  271.5 0.7 reduce_sum.188
  272.2 15.8 %all-gather.9.cloned.1.call-done = bf16[2048,1024]{1,0:T(8,128)(2,1)} async-done(((bf16[128,1024]{1,0:T(8,128)(2,1)}), bf16[2048,1024]{1,0:T(8,128)(2,1)}) %all-gather.9.cloned.1.call-update) | async-done | bytes 4194320 | tf_op jit(solution)/shard_map/all_gather | solution.py:97
  288.0 3.5 convolution_bitcast_fusion.1
  291.5 70.6 %all-gather.11.cloned.1.call-done = bf16[2048,1024]{1,0:T(8,128)(2,1)} async-done(((bf16[128,1024]{1,0:T(8,128)(2,1)}), bf16[2048,1024]{1,0:T(8,128)(2,1)}) %all-gather.11.cloned.1.call-update) | async-done | bytes 4194320 | tf_op jit(solution)/shard_map/all_gather | solution.py:98
  362.1 3.5 convolution_bitcast_fusion
  365.5 0.1 pad_maximum_fusion.1
  365.6 1.3 copy.35
  (19 shorter events, 0.2 us)
Async XLA Ops:
  7.2 86.1 %all-gather.5.cloned.1.call-start = ((), (), s32[]{:S(2)}) async-start(), calls=%async_computation.4 | async-start | bytes 4456448 | tf_op jit(solution)/shard_map/all_gather | solution.py:40
  9.1 162.2 %all-gather.7.cloned.1.call-start = ((), (), s32[]{:S(2)}) async-start(), calls=%async_computation.5 | async-start | bytes 4456448 | tf_op jit(solution)/shard_map/all_gather | solution.py:41
  40.9 133.6 %copy-start = (bf16[128,2048]{1,0:T(8,128)(2,1)S(1)}, bf16[128,2048]{1,0:T(8,128)(2,1)}, u32[]{:S(2)}) copy-start(bf16[128,2048]{1,0:T(8,128)(2,1)} %param.8) | copy-start | bytes 1572868
  40.9 133.6 %copy-start.1 = (s32[128]{0:T(128)S(1)}, s32[128]{0:T(128)}, u32[]{:S(2)}) copy-start(s32[128]{0:T(128)} %param.9) | copy-start | bytes 1540
  96.4 87.1 %copy-start.2 = (s32[1,16]{1,0:T(1,128)S(1)}, s32[1,16]{1,0:T(1,128)}, u32[]{:S(2)}) copy-start(s32[1,16]{1,0:T(1,128)} %param.11) | copy-start | bytes 196
  96.5 94.5 %copy-start.3 = (s32[1,128]{1,0:T(1,128)S(1)}, s32[1,128]{1,0:T(1,128)}, u32[]{:S(2)}) copy-start(s32[1,128]{1,0:T(1,128)} %param.10) | copy-start | bytes 1540
  176.0 14.1 %all-to-all-start = ((f32[32,8,128]{2,1,0:T(8,128)}), f32[32,8,128]{2,1,0:T(8,128)S(1)}, u32[]{:S(2)}, u32[]{:S(2)}) async-start(f32[32,8,128]{2,1,0:T(8,128)} %broadcast_in_dim.8), calls=%async_computation | async-start | bytes 262144 | tf_op jit(solution)/shard_map/all_to_all | solution.py:32
  183.5 104.5 %all-gather.9.cloned.1.call-start = ((), (), s32[]{:S(2)}) async-start(), calls=%async_computation.6 | async-start | bytes 4456448 | tf_op jit(solution)/shard_map/all_gather | solution.py:97
  193.6 168.5 %all-gather.11.cloned.1.call-start = ((), (), s32[]{:S(2)}) async-start(), calls=%async_computation.7 | async-start | bytes 4456448 | tf_op jit(solution)/shard_map/all_gather | solution.py:98
  194.1 42.0 %all-to-all-start.2 = ((bf16[128,16,128]{0,2,1:T(8,128)(2,1)}), bf16[128,16,128]{0,2,1:T(8,128)(2,1)S(1)}, u32[]{:S(2)}, u32[]{:S(2)}) async-start(bf16[128,16,128]{0,2,1:T(8,128)(2,1)} %bitcast.17), calls=%async_computation.2 | async-start | bytes 1048576 | tf_op jit(solution)/shard_map/all_to_all | solution.py:110
  236.8 20.0 %all-to-all-start.3 = ((f32[16,8,128]{2,1,0:T(8,128)}), f32[16,8,128]{2,1,0:T(8,128)S(1)}, u32[]{:S(2)}, u32[]{:S(2)}) async-start(f32[16,8,128]{2,1,0:T(8,128)} %broadcast_in_dim_broadcast_in_dim_broadcast_in_dim.3), calls=%async_computation.3 | async-start | bytes 131072 | tf_op jit(solution)/shard_map/all_to_all | solution.py:32
  256.8 14.8 %all-to-all-start.1 = ((bf16[32,128,64]{1,2,0:T(8,128)(2,1)}), bf16[32,128,64]{1,2,0:T(8,128)(2,1)S(1)}, u32[]{:S(2)}, u32[]{:S(2)}) async-start(bf16[32,128,64]{1,2,0:T(8,128)(2,1)} %bitcast.16), calls=%async_computation.1 | async-start | bytes 1048576 | tf_op jit(solution)/shard_map/all_to_all | solution.py:106
Sparse Core Ops, SparseCore 0:
  10.1 83.1 all-gather.4
  95.9 75.3 all-gather.6
  193.7 94.2 all-gather.8
  289.9 72.1 all-gather.10
where the time goes:
time: 375 us
  waiting for transfers between devices  268 us (71%)
  blocking collectives  29.9 us (8%)
  starting transfers between devices  26.5 us (7%)
  matrix products  20.8 us (6%)
  between operations  17 us (5%)
  local copies, waits for them, and re-layouts  6.89 us (2%)
  other arithmetic  5.88 us (2%)
    all_gather x1, waiting for transfers between devices, on_device(): weight_hi = lax.all_gather(head_weight[:, half:], 'dp', axis=0, tiled=True)  74.8 us
    all_gather x1, waiting for transfers between devices, on_device(): all_hi = lax.all_gather(grad_hi, 'dp', axis=0, tiled=True)  70.6 us
    all_gather x1, waiting for transfers between devices, on_device(): weight_lo = lax.all_gather(head_weight[:, :half], 'dp', axis=0, tiled=True)  52.3 us
    all_gather x1, blocking collectives, on_device(): rows_full = lax.all_gather(hidden, 'vocab', axis=1, tiled=True)  29.9 us
    all_to_all x1, waiting for transfers between devices, on_device(): lax.all_to_all(rows_full, 'dp', split_axis=1, concat_axis=0, tiled=True)  29.5 us
    all_gather x1, waiting for transfers between devices, on_device(): all_lo = lax.all_gather(grad_lo, 'dp', axis=0, tiled=True)  15.8 us
    all_to_all x2, waiting for transfers between devices, to_all(): return lax.all_to_all(copies, axis, 0, 0, tiled=True)  15.2 us
    all_to_all x2, starting transfers between devices, to_all(): return lax.all_to_all(copies, axis, 0, 0, tiled=True)  13.8 us
  transfers between devices with their start and end apart: 8, of which 8 were waited for; matrix products, arithmetic and copies ran while one was open for 5% of the time, Pallas kernels for 0%

commit v1 on v0

--- a/solution.py
+++ b/solution.py
@@ -5,6 +5,22 @@
 
 dpo_beta = 0.1
 dpo_gamma = 4.0
+
+
+def gather_around(x, axis, dim):
+    ways, here, step = (lax.axis_size(axis), lax.axis_index(axis), x.shape[dim])
+    dims = [n * ways if d == dim else n for d, n in enumerate(x.shape)]
+    full = lax.dynamic_update_slice_in_dim(jnp.zeros(dims, x.dtype), x, here * step, axis=dim)
+    going_up = going_down = x
+    for far in range(1, ways // 2 + 1):
+        going_up = lax.ppermute(going_up, axis, [(d, (d + 1) % ways) for d in range(ways)])
+        full = lax.dynamic_update_slice_in_dim(full, going_up, (here - far) % ways * step, axis=dim)
+        if 2 * far < ways:
+            going_down = lax.ppermute(going_down, axis, [(d, (d - 1) % ways) for d in range(ways)])
+            full = lax.dynamic_update_slice_in_dim(
+                full, going_down, (here + far) % ways * step, axis=dim
+            )
+    return full
 
 
 def pair_weights(log_ratio, segments, ordering):
@@ -38,7 +54,7 @@
     width = head_weight.shape[1]
     half = width // 2
     weight_lo = lax.all_gather(head_weight[:, :half], "dp", axis=0, tiled=True)
-    weight_hi = lax.all_gather(head_weight[:, half:], "dp", axis=0, tiled=True)
+    weight_hi = gather_around(head_weight[:, half:], "dp", 0)
     student = jnp.concatenate(
         [
             jnp.dot(rows_full, weight_lo, preferred_element_type=f32),

time: 375 us -> 346 us (0.923)
  the two profiles are of different devices: /device:TPU:2 before, /device:TPU:4 now
where the time goes in v1:
time: 346 us; the launch traced here: 345 us
  waiting for transfers between devices  171 us (49%)
  starting transfers between devices  84.2 us (24%)
  blocking collectives  27.1 us (8%)
  matrix products  21.2 us (6%)
  local copies, waits for them, and re-layouts  19.5 us (6%)
  between operations  17.5 us (5%)
  other arithmetic  4.84 us (1%)
    all_gather x1, waiting for transfers between devices, on_device(): all_lo = lax.all_gather(grad_lo, 'dp', axis=0, tiled=True)  72.7 us
    ppermute x7, starting transfers between devices, gather_around(): lax.ppermute(going_down, axis, [(d, (d - 1) % ways) for d in range(ways)])  39.6 us
    ppermute x8, waiting for transfers between devices, gather_around(): lax.ppermute(going_up, axis, [(d, (d + 1) % ways) for d in range(ways)])  31 us
    all_to_all x1, waiting for transfers between devices, on_device(): lax.all_to_all(rows_full, 'dp', split_axis=1, concat_axis=0, tiled=True)  29.4 us
    all_gather x1, blocking collectives, on_device(): rows_full = lax.all_gather(hidden, 'vocab', axis=1, tiled=True)  27.1 us
    ppermute x8, starting transfers between devices, gather_around(): lax.ppermute(going_up, axis, [(d, (d + 1) % ways) for d in range(ways)])  17.2 us
    all_to_all x2, waiting for transfers between devices, to_all(): return lax.all_to_all(copies, axis, 0, 0, tiled=True)  14.4 us
    all_gather x1, waiting for transfers between devices, on_device(): all_hi = lax.all_gather(grad_hi, 'dp', axis=0, tiled=True)  13.8 us
  transfers between devices with their start and end apart: 22, of which 14 were waited for; matrix products, arithmetic and copies ran while one was open for 8% of the time, Pallas kernels for 0%

profile of v1, /device:TPU:4, one launch (start us, length us, event | category | flops | bytes accessed | tf_op | source)
XLA Modules:
  0.0 344.8 jit_solution(12150652068716133115)
XLA Ops:
  7.2 2.5 broadcast_in_dim.9
  9.7 0.9 fusion.19
  10.6 3.8 %collective-permute-start = (bf16[128,1024]{1,0:T(8,128)(2,1)S(1)}, bf16[128,1024]{1,0:T(8,128)(2,1)S(1)}, u32[]{:S(2)}, u32[]{:S(2)}) collective-permute-start(bf16[128,1024]{1,0:T(8,128)(2,1)S(1)} %get-tuple-element.29), channel_id=1, source_target_pairs={{0,1},{1,2},{2,3},{3,4},{4,5},{5,6},{6,7},{7,8},{8,9},{9,10},{10,1... | collective-permute-start | bytes 786440 | tf_op jit(solution)/shard_map/ppermute | solution.py:16
  14.5 9.5 %collective-permute-start.1 = (bf16[128,1024]{1,0:T(8,128)(2,1)S(1)}, bf16[128,1024]{1,0:T(8,128)(2,1)S(1)}, u32[]{:S(2)}, u32[]{:S(2)}) collective-permute-start(bf16[128,1024]{1,0:T(8,128)(2,1)S(1)} %get-tuple-element.29), channel_id=1, source_target_pairs={{0,15},{1,0},{2,1},{3,2},{4,3},{5,4},{6,5},{7,6},{8,7},{9,8},{10,9... | collective-permute-start | bytes 786440 | tf_op jit(solution)/shard_map/ppermute | solution.py:19
  24.0 4.4 %collective-permute-done = bf16[128,1024]{1,0:T(8,128)(2,1)S(1)} collective-permute-done((bf16[128,1024]{1,0:T(8,128)(2,1)S(1)}, bf16[128,1024]{1,0:T(8,128)(2,1)S(1)}, u32[]{:S(2)}, u32[]{:S(2)}) %collective-permute-start) | collective-permute-done | bytes 262176 | tf_op jit(solution)/shard_map/ppermute | solution.py:16
  28.4 1.9 collective-permute-start.2
  30.3 5.1 %collective-permute-start.3 = (bf16[128,1024]{1,0:T(8,128)(2,1)S(1)}, bf16[128,1024]{1,0:T(8,128)(2,1)S(1)}, u32[]{:S(2)}, u32[]{:S(2)}) collective-permute-start(bf16[128,1024]{1,0:T(8,128)(2,1)S(1)} %collective-permute-done.1), channel_id=1, source_target_pairs={{0,15},{1,0},{2,1},{3,2},{4,3},{5,4},{6,5},{7,6},{8,7},{9,8},{10,9... | collective-permute-start | bytes 786440 | tf_op jit(solution)/shard_map/ppermute | solution.py:19
  35.6 8.1 %collective-permute-done.2 = bf16[128,1024]{1,0:T(8,128)(2,1)S(1)} collective-permute-done((bf16[128,1024]{1,0:T(8,128)(2,1)S(1)}, bf16[128,1024]{1,0:T(8,128)(2,1)S(1)}, u32[]{:S(2)}, u32[]{:S(2)}) %collective-permute-start.2) | collective-permute-done | bytes 262176 | tf_op jit(solution)/shard_map/ppermute | solution.py:16
  43.7 1.9 collective-permute-start.4
  46.3 4.5 %collective-permute-start.5 = (bf16[128,1024]{1,0:T(8,128)(2,1)S(1)}, bf16[128,1024]{1,0:T(8,128)(2,1)S(1)}, u32[]{:S(2)}, u32[]{:S(2)}) collective-permute-start(bf16[128,1024]{1,0:T(8,128)(2,1)S(1)} %collective-permute-done.3), channel_id=1, source_target_pairs={{0,15},{1,0},{2,1},{3,2},{4,3},{5,4},{6,5},{7,6},{8,7},{9,8},{10,9... | collective-permute-start | bytes 786440 | tf_op jit(solution)/shard_map/ppermute | solution.py:19
  50.8 27.1 %all_gather.12 = bf16[128,2048]{0,1:T(8,128)(2,1)} all-gather(bf16[128,64]{0,1:T(8,128)(2,1)S(1)} %copy-done.2), channel_id=1, replica_groups=mesh['vocab'=32,'dp'=16] {'vocab'}, dimensions={1}, use_global_device_ids=true | all-gather | bytes 540672 | tf_op jit(solution)/shard_map/all_gather | solution.py:53
  77.9 1.9 collective-permute-start.6
  80.9 5.1 %collective-permute-start.7 = (bf16[128,1024]{1,0:T(8,128)(2,1)S(1)}, bf16[128,1024]{1,0:T(8,128)(2,1)S(1)}, u32[]{:S(2)}, u32[]{:S(2)}) collective-permute-start(bf16[128,1024]{1,0:T(8,128)(2,1)S(1)} %collective-permute-done.5), channel_id=1, source_target_pairs={{0,15},{1,0},{2,1},{3,2},{4,3},{5,4},{6,5},{7,6},{8,7},{9,8},{10,9... | collective-permute-start | bytes 786440 | tf_op jit(solution)/shard_map/ppermute | solution.py:19
  86.0 0.7 constant_dynamic-update-slice_fusion.13
  86.7 8.4 %collective-permute-done.6 = bf16[128,1024]{1,0:T(8,128)(2,1)S(1)} collective-permute-done((bf16[128,1024]{1,0:T(8,128)(2,1)S(1)}, bf16[128,1024]{1,0:T(8,128)(2,1)S(1)}, u32[]{:S(2)}, u32[]{:S(2)}) %collective-permute-start.6) | collective-permute-done | bytes 262176 | tf_op jit(solution)/shard_map/ppermute | solution.py:16
  95.2 1.9 collective-permute-start.8
  97.8 0.7 constant_dynamic-update-slice_fusion.11
  98.6 5.1 %collective-permute-start.9 = (bf16[128,1024]{1,0:T(8,128)(2,1)S(1)}, bf16[128,1024]{1,0:T(8,128)(2,1)S(1)}, u32[]{:S(2)}, u32[]{:S(2)}) collective-permute-start(bf16[128,1024]{1,0:T(8,128)(2,1)S(1)} %collective-permute-done.7), channel_id=1, source_target_pairs={{0,15},{1,0},{2,1},{3,2},{4,3},{5,4},{6,5},{7,6},{8,7},{9,8},{10,9... | collective-permute-start | bytes 786440 | tf_op jit(solution)/shard_map/ppermute | solution.py:19
  103.7 0.7 constant_dynamic-update-slice_fusion.10
  104.4 2.7 collective-permute-done.8
  107.1 1.9 collective-permute-start.10
  110.5 5.1 %collective-permute-start.11 = (bf16[128,1024]{1,0:T(8,128)(2,1)S(1)}, bf16[128,1024]{1,0:T(8,128)(2,1)S(1)}, u32[]{:S(2)}, u32[]{:S(2)}) collective-permute-start(bf16[128,1024]{1,0:T(8,128)(2,1)S(1)} %collective-permute-done.9), channel_id=1, source_target_pairs={{0,15},{1,0},{2,1},{3,2},{4,3},{5,4},{6,5},{7,6},{8,7},{9,8},{10,9... | collective-permute-start | bytes 786440 | tf_op jit(solution)/shard_map/ppermute | solution.py:19
  116.3 1.5 collective-permute-done.10
  117.8 1.9 collective-permute-start.12
  121.1 5.1 %collective-permute-start.13 = (bf16[128,1024]{1,0:T(8,128)(2,1)S(1)}, bf16[128,1024]{1,0:T(8,128)(2,1)S(1)}, u32[]{:S(2)}, u32[]{:S(2)}) collective-permute-start(bf16[128,1024]{1,0:T(8,128)(2,1)S(1)} %collective-permute-done.11), channel_id=1, source_target_pairs={{0,15},{1,0},{2,1},{3,2},{4,3},{5,4},{6,5},{7,6},{8,7},{9,8},{10,9... | collective-permute-start | bytes 786440 | tf_op jit(solution)/shard_map/ppermute | solution.py:19
  126.3 0.7 constant_dynamic-update-slice_fusion.4
  127.6 1.9 collective-permute-start.14
  131.7 5.4 %collective-permute-done.14 = bf16[128,1024]{1,0:T(8,128)(2,1)S(1)} collective-permute-done((bf16[128,1024]{1,0:T(8,128)(2,1)S(1)}, bf16[128,1024]{1,0:T(8,128)(2,1)S(1)}, u32[]{:S(2)}, u32[]{:S(2)}) %collective-permute-start.14) | collective-permute-done | bytes 262176 | tf_op jit(solution)/shard_map/ppermute | solution.py:16
  137.8 3.6 %fusion.23 = (f32[128]{0:T(128)S(1)}, f32[1024,128]{1,0:T(8,128)S(1)}) fusion(bf16[2048,1024]{1,0:T(8,128)(2,1)} %constant_dynamic-update-slice_fusion, bf16[128,2048]{0,1:T(8,128)(2,1)} %all_gather.12), kind=kOutput, calls=%fused_computation.73 | convolution fusion | flops 537001856 | bytes 5243392 | tf_op jit(solution)/shard_map/dot_general | solution.py:61
  141.6 3.2 fusion.22
  144.8 0.8 fusion.1
  146.3 5.8 %all-to-all-start = ((f32[32,8,128]{2,1,0:T(8,128)}), f32[32,8,128]{2,1,0:T(8,128)S(1)}, u32[]{:S(2)}, u32[]{:S(2)}) async-start(f32[32,8,128]{2,1,0:T(8,128)} %broadcast_in_dim.11), calls=%async_computation | async-start | bytes 262144 | tf_op jit(solution)/shard_map/all_to_all | solution.py:48
  152.4 5.6 %all-to-all-done = f32[32,8,128]{2,1,0:T(8,128)S(1)} async-done(((f32[32,8,128]{2,1,0:T(8,128)}), f32[32,8,128]{2,1,0:T(8,128)S(1)}, u32[]{:S(2)}, u32[]{:S(2)}) %all-to-all-start) | async-done | bytes 131104 | tf_op jit(solution)/shard_map/all_to_all | solution.py:48
  160.5 0.8 fusion.18
  162.2 8.7 %all-to-all-start.2 = ((bf16[128,16,128]{0,2,1:T(8,128)(2,1)}), bf16[128,16,128]{0,2,1:T(8,128)(2,1)S(1)}, u32[]{:S(2)}, u32[]{:S(2)}) async-start(bf16[128,16,128]{0,2,1:T(8,128)(2,1)} %bitcast.18), calls=%async_computation.2 | async-start | bytes 1048576 | tf_op jit(solution)/shard_map/all_to_all | solution.py:126
  172.1 3.8 %fusion.16 = f32[128,2048]{1,0:T(8,128)S(1)} fusion(bf16[2048,1024]{1,0:T(8,128)(2,1)} %all-gather.4.cloned.1.call-done, bf16[128,2048]{1,0:T(8,128)(2,1)S(1)} %fusion.5), kind=kOutput, calls=%fused_computation.66 | convolution fusion | flops 536870912 | bytes 5505024 | tf_op jit(solution)/shard_map/dot_general | solution.py:117
  175.9 29.4 %all-to-all-done.2 = bf16[128,16,128]{0,2,1:T(8,128)(2,1)S(1)} async-done(((bf16[128,16,128]{0,2,1:T(8,128)(2,1)}), bf16[128,16,128]{0,2,1:T(8,128)(2,1)S(1)}, u32[]{:S(2)}, u32[]{:S(2)}) %all-to-all-start.2) | async-done | bytes 524320 | tf_op jit(solution)/shard_map/all_to_all | solution.py:126
  205.9 6.4 %all-to-all-start.3 = ((f32[16,8,128]{2,1,0:T(8,128)}), f32[16,8,128]{2,1,0:T(8,128)S(1)}, u32[]{:S(2)}, u32[]{:S(2)}) async-start(f32[16,8,128]{2,1,0:T(8,128)} %broadcast_in_dim_broadcast_in_dim_broadcast_in_dim.3), calls=%async_computation.3 | async-start | bytes 131072 | tf_op jit(solution)/shard_map/all_to_all | solution.py:48
  212.4 3.7 %fusion = bf16[128,2048]{1,0:T(8,128)(2,1)S(1)} fusion(f32[128,2048]{1,0:T(8,128)S(1)} %fusion.16, bf16[2048,1024]{1,0:T(8,128)(2,1)} %constant_dynamic-update-slice_fusion, bf16[128,2048]{1,0:T(8,128)(2,1)S(1)} %fusion.5), kind=kOutput, calls=%fused_computation.1 | convolution fusion | flops 537395200 | bytes 6029312 | tf_op jit(solution)/shard_map/dot_general | solution.py:118
  216.1 1.0 copy.37
  217.1 8.8 %all-to-all-done.3 = f32[16,8,128]{2,1,0:T(8,128)S(1)} async-done(((f32[16,8,128]{2,1,0:T(8,128)}), f32[16,8,128]{2,1,0:T(8,128)S(1)}, u32[]{:S(2)}, u32[]{:S(2)}) %all-to-all-start.3) | async-done | bytes 65568 | tf_op jit(solution)/shard_map/all_to_all | solution.py:48
  225.9 6.3 %all-to-all-start.1 = ((bf16[32,128,64]{1,2,0:T(8,128)(2,1)}), bf16[32,128,64]{1,2,0:T(8,128)(2,1)S(1)}, u32[]{:S(2)}, u32[]{:S(2)}) async-start(bf16[32,128,64]{1,2,0:T(8,128)(2,1)} %bitcast.17), calls=%async_computation.1 | async-start | bytes 1048576 | tf_op jit(solution)/shard_map/all_to_all | solution.py:122
  233.8 7.9 %all-to-all-done.1 = bf16[32,128,64]{1,2,0:T(8,128)(2,1)S(1)} async-done(((bf16[32,128,64]{1,2,0:T(8,128)(2,1)}), bf16[32,128,64]{1,2,0:T(8,128)(2,1)S(1)}, u32[]{:S(2)}, u32[]{:S(2)}) %all-to-all-start.1) | async-done | bytes 524320 | tf_op jit(solution)/shard_map/all_to_all | solution.py:122
  242.4 13.8 %all-gather.8.cloned.1.call-done = bf16[2048,1024]{1,0:T(8,128)(2,1)} async-done(((bf16[128,1024]{1,0:T(8,128)(2,1)}), bf16[2048,1024]{1,0:T(8,128)(2,1)}) %all-gather.8.cloned.1.call-update) | async-done | bytes 4194320 | tf_op jit(solution)/shard_map/all_gather | solution.py:114
  256.2 3.5 %convolution_bitcast_fusion = f32[128,1024]{0,1:T(8,128)S(1)} fusion(bf16[2048,1024]{1,0:T(8,128)(2,1)} %all-gather.8.cloned.1.call-done, bf16[2048,128]{1,0:T(8,128)(2,1)S(1)} %bitcast.46), kind=kOutput, calls=%fused_computation.8 | convolution fusion | flops 536870912 | bytes 5242880 | tf_op jit(solution)/shard_map/dot_general | solution.py:131
  259.7 72.7 %all-gather.6.cloned.1.call-done = bf16[2048,1024]{1,0:T(8,128)(2,1)} async-done(((bf16[128,1024]{1,0:T(8,128)(2,1)}), bf16[2048,1024]{1,0:T(8,128)(2,1)}) %all-gather.6.cloned.1.call-update) | async-done | bytes 4194320 | tf_op jit(solution)/shard_map/all_gather | solution.py:113
  332.3 3.5 %convolution_bitcast_fusion.1 = f32[128,1024]{0,1:T(8,128)S(1)} fusion(bf16[2048,1024]{1,0:T(8,128)(2,1)} %all-gather.6.cloned.1.call-done, bf16[2048,128]{1,0:T(8,128)(2,1)S(1)} %bitcast.47), kind=kOutput, calls=%fused_computation.9 | convolution fusion | flops 536870912 | bytes 5242880 | tf_op jit(solution)/shard_map/dot_general | solution.py:130
  335.9 1.3 copy.40
  (67 shorter events, 16.1 us)
Async XLA Ops:
  7.2 2.6 copy-start.1
  7.2 28.2 %copy-start = (bf16[128,2048]{1,0:T(8,128)(2,1)S(1)}, bf16[128,2048]{1,0:T(8,128)(2,1)}, u32[]{:S(2)}) copy-start(bf16[128,2048]{1,0:T(8,128)(2,1)} %param.8) | copy-start | bytes 1572868
  7.2 43.6 %copy-start.2 = (bf16[128,64]{0,1:T(8,128)(2,1)S(1)}, bf16[128,64]{0,1:T(8,128)(2,1)}, u32[]{:S(2)}) copy-start(bf16[128,64]{0,1:T(8,128)(2,1)} %param.6) | copy-start | bytes 49156
  7.2 134.4 %all-gather.4.cloned.1.call-start = ((), (), s32[]{:S(2)}) async-start(), calls=%async_computation.4 | async-start | bytes 4456448 | tf_op jit(solution)/shard_map/all_gather | solution.py:56
  10.6 17.7 %collective-permute-start = (bf16[128,1024]{1,0:T(8,128)(2,1)S(1)}, bf16[128,1024]{1,0:T(8,128)(2,1)S(1)}, u32[]{:S(2)}, u32[]{:S(2)}) collective-permute-start(bf16[128,1024]{1,0:T(8,128)(2,1)S(1)} %get-tuple-element.29), channel_id=1, source_target_pairs={{0,1},{1,2},{2,3},{3,4},{4,5},{5,6},{6,7},{7,8},{8,9},{9,10},{10,1... | collective-permute-start | bytes 786440 | tf_op jit(solution)/shard_map/ppermute | solution.py:16
  14.5 15.8 %collective-permute-start.1 = (bf16[128,1024]{1,0:T(8,128)(2,1)S(1)}, bf16[128,1024]{1,0:T(8,128)(2,1)S(1)}, u32[]{:S(2)}, u32[]{:S(2)}) collective-permute-start(bf16[128,1024]{1,0:T(8,128)(2,1)S(1)} %get-tuple-element.29), channel_id=1, source_target_pairs={{0,15},{1,0},{2,1},{3,2},{4,3},{5,4},{6,5},{7,6},{8,7},{9,8},{10,9... | collective-permute-start | bytes 786440 | tf_op jit(solution)/shard_map/ppermute | solution.py:19
  28.4 15.3 %collective-permute-start.2 = (bf16[128,1024]{1,0:T(8,128)(2,1)S(1)}, bf16[128,1024]{1,0:T(8,128)(2,1)S(1)}, u32[]{:S(2)}, u32[]{:S(2)}) collective-permute-start(bf16[128,1024]{1,0:T(8,128)(2,1)S(1)} %collective-permute-done), channel_id=1, source_target_pairs={{0,1},{1,2},{2,3},{3,4},{4,5},{5,6},{6,7},{7,8},{8,9},{9,10},{10,1... | collective-permute-start | bytes 786440 | tf_op jit(solution)/shard_map/ppermute | solution.py:16
  30.3 16.0 %collective-permute-start.3 = (bf16[128,1024]{1,0:T(8,128)(2,1)S(1)}, bf16[128,1024]{1,0:T(8,128)(2,1)S(1)}, u32[]{:S(2)}, u32[]{:S(2)}) collective-permute-start(bf16[128,1024]{1,0:T(8,128)(2,1)S(1)} %collective-permute-done.1), channel_id=1, source_target_pairs={{0,15},{1,0},{2,1},{3,2},{4,3},{5,4},{6,5},{7,6},{8,7},{9,8},{10,9... | collective-permute-start | bytes 786440 | tf_op jit(solution)/shard_map/ppermute | solution.py:19
  43.7 34.2 %collective-permute-start.4 = (bf16[128,1024]{1,0:T(8,128)(2,1)S(1)}, bf16[128,1024]{1,0:T(8,128)(2,1)S(1)}, u32[]{:S(2)}, u32[]{:S(2)}) collective-permute-start(bf16[128,1024]{1,0:T(8,128)(2,1)S(1)} %collective-permute-done.2), channel_id=1, source_target_pairs={{0,1},{1,2},{2,3},{3,4},{4,5},{5,6},{6,7},{7,8},{8,9},{9,10},{10,1... | collective-permute-start | bytes 786440 | tf_op jit(solution)/shard_map/ppermute | solution.py:16
  46.3 34.6 %collective-permute-start.5 = (bf16[128,1024]{1,0:T(8,128)(2,1)S(1)}, bf16[128,1024]{1,0:T(8,128)(2,1)S(1)}, u32[]{:S(2)}, u32[]{:S(2)}) collective-permute-start(bf16[128,1024]{1,0:T(8,128)(2,1)S(1)} %collective-permute-done.3), channel_id=1, source_target_pairs={{0,15},{1,0},{2,1},{3,2},{4,3},{5,4},{6,5},{7,6},{8,7},{9,8},{10,9... | collective-permute-start | bytes 786440 | tf_op jit(solution)/shard_map/ppermute | solution.py:19
  77.9 17.2 %collective-permute-start.6 = (bf16[128,1024]{1,0:T(8,128)(2,1)S(1)}, bf16[128,1024]{1,0:T(8,128)(2,1)S(1)}, u32[]{:S(2)}, u32[]{:S(2)}) collective-permute-start(bf16[128,1024]{1,0:T(8,128)(2,1)S(1)} %collective-permute-done.4), channel_id=1, source_target_pairs={{0,1},{1,2},{2,3},{3,4},{4,5},{5,6},{6,7},{7,8},{8,9},{9,10},{10,1... | collective-permute-start | bytes 786440 | tf_op jit(solution)/shard_map/ppermute | solution.py:16
  80.9 17.7 %collective-permute-start.7 = (bf16[128,1024]{1,0:T(8,128)(2,1)S(1)}, bf16[128,1024]{1,0:T(8,128)(2,1)S(1)}, u32[]{:S(2)}, u32[]{:S(2)}) collective-permute-start(bf16[128,1024]{1,0:T(8,128)(2,1)S(1)} %collective-permute-done.5), channel_id=1, source_target_pairs={{0,15},{1,0},{2,1},{3,2},{4,3},{5,4},{6,5},{7,6},{8,7},{9,8},{10,9... | collective-permute-start | bytes 786440 | tf_op jit(solution)/shard_map/ppermute | solution.py:19
  95.2 11.9 %collective-permute-start.8 = (bf16[128,1024]{1,0:T(8,128)(2,1)S(1)}, bf16[128,1024]{1,0:T(8,128)(2,1)S(1)}, u32[]{:S(2)}, u32[]{:S(2)}) collective-permute-start(bf16[128,1024]{1,0:T(8,128)(2,1)S(1)} %collective-permute-done.6), channel_id=1, source_target_pairs={{0,1},{1,2},{2,3},{3,4},{4,5},{5,6},{6,7},{7,8},{8,9},{9,10},{10,1... | collective-permute-start | bytes 786440 | tf_op jit(solution)/shard_map/ppermute | solution.py:16
  98.6 11.9 %collective-permute-start.9 = (bf16[128,1024]{1,0:T(8,128)(2,1)S(1)}, bf16[128,1024]{1,0:T(8,128)(2,1)S(1)}, u32[]{:S(2)}, u32[]{:S(2)}) collective-permute-start(bf16[128,1024]{1,0:T(8,128)(2,1)S(1)} %collective-permute-done.7), channel_id=1, source_target_pairs={{0,15},{1,0},{2,1},{3,2},{4,3},{5,4},{6,5},{7,6},{8,7},{9,8},{10,9... | collective-permute-start | bytes 786440 | tf_op jit(solution)/shard_map/ppermute | solution.py:19
  107.1 10.7 %collective-permute-start.10 = (bf16[128,1024]{1,0:T(8,128)(2,1)S(1)}, bf16[128,1024]{1,0:T(8,128)(2,1)S(1)}, u32[]{:S(2)}, u32[]{:S(2)}) collective-permute-start(bf16[128,1024]{1,0:T(8,128)(2,1)S(1)} %collective-permute-done.8), channel_id=1, source_target_pairs={{0,1},{1,2},{2,3},{3,4},{4,5},{5,6},{6,7},{7,8},{8,9},{9,10},{10,1... | collective-permute-start | bytes 786440 | tf_op jit(solution)/shard_map/ppermute | solution.py:16
  110.5 10.7 %collective-permute-start.11 = (bf16[128,1024]{1,0:T(8,128)(2,1)S(1)}, bf16[128,1024]{1,0:T(8,128)(2,1)S(1)}, u32[]{:S(2)}, u32[]{:S(2)}) collective-permute-start(bf16[128,1024]{1,0:T(8,128)(2,1)S(1)} %collective-permute-done.9), channel_id=1, source_target_pairs={{0,15},{1,0},{2,1},{3,2},{4,3},{5,4},{6,5},{7,6},{8,7},{9,8},{10,9... | collective-permute-start | bytes 786440 | tf_op jit(solution)/shard_map/ppermute | solution.py:19
  117.8 9.8 %collective-permute-start.12 = (bf16[128,1024]{1,0:T(8,128)(2,1)S(1)}, bf16[128,1024]{1,0:T(8,128)(2,1)S(1)}, u32[]{:S(2)}, u32[]{:S(2)}) collective-permute-start(bf16[128,1024]{1,0:T(8,128)(2,1)S(1)} %collective-permute-done.10), channel_id=1, source_target_pairs={{0,1},{1,2},{2,3},{3,4},{4,5},{5,6},{6,7},{7,8},{8,9},{9,10},{10,1... | collective-permute-start | bytes 786440 | tf_op jit(solution)/shard_map/ppermute | solution.py:16
  121.1 9.8 %collective-permute-start.13 = (bf16[128,1024]{1,0:T(8,128)(2,1)S(1)}, bf16[128,1024]{1,0:T(8,128)(2,1)S(1)}, u32[]{:S(2)}, u32[]{:S(2)}) collective-permute-start(bf16[128,1024]{1,0:T(8,128)(2,1)S(1)} %collective-permute-done.11), channel_id=1, source_target_pairs={{0,15},{1,0},{2,1},{3,2},{4,3},{5,4},{6,5},{7,6},{8,7},{9,8},{10,9... | collective-permute-start | bytes 786440 | tf_op jit(solution)/shard_map/ppermute | solution.py:19
  127.6 9.5 %collective-permute-start.14 = (bf16[128,1024]{1,0:T(8,128)(2,1)S(1)}, bf16[128,1024]{1,0:T(8,128)(2,1)S(1)}, u32[]{:S(2)}, u32[]{:S(2)}) collective-permute-start(bf16[128,1024]{1,0:T(8,128)(2,1)S(1)} %collective-permute-done.12), channel_id=1, source_target_pairs={{0,1},{1,2},{2,3},{3,4},{4,5},{5,6},{6,7},{7,8},{8,9},{9,10},{10,1... | collective-permute-start | bytes 786440 | tf_op jit(solution)/shard_map/ppermute | solution.py:16
  141.3 3.5 %copy-start.3 = (s32[128]{0:T(128)S(1)}, s32[128]{0:T(128)}, u32[]{:S(2)}) copy-start(s32[128]{0:T(128)} %param.9) | copy-start | bytes 1540
  141.4 10.8 %copy-start.4 = (s32[1,16]{1,0:T(1,128)S(1)}, s32[1,16]{1,0:T(1,128)}, u32[]{:S(2)}) copy-start(s32[1,16]{1,0:T(1,128)} %param.11) | copy-start | bytes 196
  141.4 17.4 %copy-start.5 = (s32[1,128]{1,0:T(1,128)S(1)}, s32[1,128]{1,0:T(1,128)}, u32[]{:S(2)}) copy-start(s32[1,128]{1,0:T(1,128)} %param.10) | copy-start | bytes 1540
  146.3 11.7 %all-to-all-start = ((f32[32,8,128]{2,1,0:T(8,128)}), f32[32,8,128]{2,1,0:T(8,128)S(1)}, u32[]{:S(2)}, u32[]{:S(2)}) async-start(f32[32,8,128]{2,1,0:T(8,128)} %broadcast_in_dim.11), calls=%async_computation | async-start | bytes 262144 | tf_op jit(solution)/shard_map/all_to_all | solution.py:48
  152.2 104.0 %all-gather.8.cloned.1.call-start = ((), (), s32[]{:S(2)}) async-start(), calls=%async_computation.6 | async-start | bytes 4456448 | tf_op jit(solution)/shard_map/all_gather | solution.py:114
  161.4 170.9 %all-gather.6.cloned.1.call-start = ((), (), s32[]{:S(2)}) async-start(), calls=%async_computation.5 | async-start | bytes 4456448 | tf_op jit(solution)/shard_map/all_gather | solution.py:113
  162.2 43.2 %all-to-all-start.2 = ((bf16[128,16,128]{0,2,1:T(8,128)(2,1)}), bf16[128,16,128]{0,2,1:T(8,128)(2,1)S(1)}, u32[]{:S(2)}, u32[]{:S(2)}) async-start(bf16[128,16,128]{0,2,1:T(8,128)(2,1)} %bitcast.18), calls=%async_computation.2 | async-start | bytes 1048576 | tf_op jit(solution)/shard_map/all_to_all | solution.py:126
  205.9 20.0 %all-to-all-start.3 = ((f32[16,8,128]{2,1,0:T(8,128)}), f32[16,8,128]{2,1,0:T(8,128)S(1)}, u32[]{:S(2)}, u32[]{:S(2)}) async-start(f32[16,8,128]{2,1,0:T(8,128)} %broadcast_in_dim_broadcast_in_dim_broadcast_in_dim.3), calls=%async_computation.3 | async-start | bytes 131072 | tf_op jit(solution)/shard_map/all_to_all | solution.py:48
  225.9 15.8 %all-to-all-start.1 = ((bf16[32,128,64]{1,2,0:T(8,128)(2,1)}), bf16[32,128,64]{1,2,0:T(8,128)(2,1)S(1)}, u32[]{:S(2)}, u32[]{:S(2)}) async-start(bf16[32,128,64]{1,2,0:T(8,128)(2,1)} %bitcast.17), calls=%async_computation.1 | async-start | bytes 1048576 | tf_op jit(solution)/shard_map/all_to_all | solution.py:122
Sparse Core Ops, SparseCore 0:
  10.8 93.1 all-gather.3
  161.5 94.6 all-gather.7
  258.3 73.9 all-gather.5
